TPU v7x, 256 devices: a whole 4x4x8 slice. The times are simulated.
256 devices in a mesh: grp: 2 (over core), row: 4 (over x), col: 32 (over z, y).
Axes of the slice: x: 4, y: 4, z: 8, core: 2. Of those that a mesh axis runs over, the one named last changes fastest.
Arguments:
- front_matrix: float32 [2, 8192, 8192], P('grp', 'row', 'col'), may hold values from -1 to 41
- row_pattern: int32 [2, 64], replicated, may hold values from 0 to 1, as said below
- col_pattern: int32 [2, 64], replicated, may hold values from 0 to 1, as said below
Outputs:
- contribution: float32 [8192, 8192], P('row', 'col')
Inputs may be any that keep to these rules, and one draw needn't show every extreme that they name: `row_pattern`: entries are 0 or 1; entries 0 and 1 of each row are 1. `col_pattern`: entries are 0 or 1; entries 0 and 1 of each row are 1.
All inputs are finite; a program needn't handle non-finite values.
Results may differ from a plain program's by a relative error of at most 0.0001.
Values sent between devices are 32-bit elements; how exact they have to be, the bound alone decides.
A program may use at most 64 MiB of HBM per device.

v0:
```python
import jax
import jax.numpy as jnp
from jax import lax
from jax.sharding import PartitionSpec as P

B = 128
STEPS = 2


def spread(block, axis, owner):
    block = jnp.where(lax.axis_index(axis) == owner, block, jnp.zeros_like(block))
    return lax.psum(block, axis)


def invert_lower(lower_unit):
    highest = lax.Precision.HIGHEST
    extent = lower_unit.shape[0]
    places = jnp.arange(extent, dtype=jnp.int32)
    basis = jnp.eye(extent, dtype=jnp.float32)

    def sweep(index, result):
        line = lax.dynamic_index_in_dim(lower_unit, index, 0, keepdims=False)
        coeffs = jnp.where(places < index, line, 0.0)
        unit_row = lax.dynamic_index_in_dim(basis, index, 0, keepdims=False)
        row_new = unit_row - jnp.dot(coeffs, result, precision=highest)
        return lax.dynamic_update_slice_in_dim(result, row_new[None, :], index, 0)

    return lax.fori_loop(0, extent, sweep, basis)


def invert_upper(upper_tri):
    highest = lax.Precision.HIGHEST
    extent = upper_tri.shape[0]
    places = jnp.arange(extent, dtype=jnp.int32)
    basis = jnp.eye(extent, dtype=jnp.float32)

    def sweep(count, result):
        index = extent - 1 - count
        line = lax.dynamic_index_in_dim(upper_tri, index, 0, keepdims=False)
        coeffs = jnp.where(places > index, line, 0.0)
        pivot_value = jnp.sum(jnp.where(places == index, line, 0.0))
        unit_row = lax.dynamic_index_in_dim(basis, index, 0, keepdims=False)
        row_new = (unit_row - jnp.dot(coeffs, result, precision=highest)) / pivot_value
        return lax.dynamic_update_slice_in_dim(result, row_new[None, :], index, 0)

    return lax.fori_loop(0, extent, sweep, jnp.zeros((extent, extent), jnp.float32))


def factor_block(block):
    highest = lax.Precision.HIGHEST
    extent = block.shape[0]
    tile = min(32, extent)
    packed = block
    for first in range(0, extent, tile):
        height = extent - first
        row_places = jnp.arange(height, dtype=jnp.int32)
        col_places = jnp.arange(tile, dtype=jnp.int32)

        def sweep(k, panel):
            pivot_value = panel[k, k]
            below_col = jnp.where(row_places > k, panel[:, k] / pivot_value, 0.0)
            right_row = jnp.where(col_places > k, panel[k, :], 0.0)
            panel = panel - below_col[:, None] * right_row[None, :]
            panel = jnp.where(
                (col_places[None, :] == k) & (row_places[:, None] > k), below_col[:, None], panel
            )
            return panel

        panel = lax.fori_loop(0, tile, sweep, packed[first:, first : first + tile])
        packed = packed.at[first:, first : first + tile].set(panel)
        if first + tile < extent:
            tile_lower = jnp.tril(panel[:tile], -1) + jnp.eye(tile, dtype=panel.dtype)
            tile_inverse = invert_lower(tile_lower)
            row_part = jnp.dot(
                tile_inverse, packed[first : first + tile, first + tile :], precision=highest
            )
            packed = packed.at[first : first + tile, first + tile :].set(row_part)
            update = jnp.dot(panel[tile:], row_part, precision=highest)
            packed = packed.at[first + tile :, first + tile :].add(-update)
    lower_unit = jnp.tril(packed, -1) + jnp.eye(extent, dtype=packed.dtype)
    upper_tri = jnp.triu(packed)
    return (lower_unit, upper_tri)


def shards(front_matrix, row_pattern, col_pattern):
    highest = lax.Precision.HIGHEST
    working = front_matrix[0]
    rows_here = working.shape[0] // B
    cols_here = working.shape[1] // B
    row_start = lax.axis_index("row") * rows_here
    col_start = lax.axis_index("col") * cols_here
    row_blocks = row_start + jnp.arange(working.shape[0], dtype=jnp.int32) // B
    col_blocks = col_start + jnp.arange(working.shape[1], dtype=jnp.int32) // B
    for k in range(STEPS):
        keep_rows = jnp.repeat(lax.dynamic_slice_in_dim(row_pattern[k], row_start, rows_here), B)
        keep_cols = jnp.repeat(lax.dynamic_slice_in_dim(col_pattern[k], col_start, cols_here), B)
        working = jnp.where((col_blocks == k)[None, :] & (keep_rows == 0)[:, None], 0.0, working)
        working = jnp.where((row_blocks == k)[:, None] & (keep_cols == 0)[None, :], 0.0, working)
    for k in range(STEPS):
        corner = spread(working[k * B : (k + 1) * B, k * B : (k + 1) * B], ("row", "col"), 0)
        lower_unit, upper_tri = factor_block(corner)
        lower_rows = jnp.dot(
            working[:, k * B : (k + 1) * B], invert_upper(upper_tri), precision=highest
        )
        lower_rows = jnp.where((row_blocks > k)[:, None], lower_rows, 0.0)
        lower_rows = spread(lower_rows, "col", 0)
        upper_cols = jnp.dot(
            invert_lower(lower_unit), working[k * B : (k + 1) * B, :], precision=highest
        )
        upper_cols = jnp.where((col_blocks > k)[None, :], upper_cols, 0.0)
        upper_cols = spread(upper_cols, "row", 0)
        working = working - jnp.dot(lower_rows, upper_cols, precision=highest)
    trailing = (row_blocks >= STEPS)[:, None] & (col_blocks >= STEPS)[None, :]
    partial_update = jnp.where(trailing, working, 0.0)
    return lax.psum(partial_update, "grp")


def solution(mesh):
    in_specs = (P("grp", "row", "col"), P(), P())
    out_specs = P("row", "col")
    return jax.shard_map(shards, mesh=mesh, in_specs=in_specs, out_specs=out_specs, check_vma=False)
```

profile of v0, /device:TPU:37, one launch (start us, length us, event | category | flops | bytes accessed | tf_op | source)
XLA Modules:
  0.0 1767.9 jit_solution(10045455909963875308)
XLA Ops:
  8.5 3.6 fusion.177
  14.5 205.4 %all-reduce.8.cloned.1.call-done = f32[128,128]{1,0:T(8,128)} async-done(((f32[128,128]{1,0:T(8,128)}), f32[128,128]{1,0:T(8,128)}) %all-reduce.8.cloned.1.call-update) | async-done | bytes 65552 | tf_op jit(solution)/shard_map/psum | solution.py:12
  220.8 45.0 %while.296 = (s32[]{:T(128)}, f32[128,32]{0,1:T(8,128)S(1)}, s32[]{:T(128)}) while((s32[]{:T(128)}, f32[128,32]{0,1:T(8,128)S(1)}, s32[]{:T(128)}) %tuple.637), condition=%wide.region_3.4_spmd.clone.clone, body=%wide.region_2.3_spmd.clone.clone.sunk | while | flops 16994 | bytes 69901 | solution.py:69
  265.9 5.6 while.288
  274.5 2.9 dynamic-slice_select_fusion.1
  277.5 3.6 scatter.49
  284.1 44.7 %while.297 = (s32[]{:T(128)}, f32[96,32]{0,1:T(8,128)S(1)}, s32[]{:T(128)}) while((s32[]{:T(128)}, f32[96,32]{0,1:T(8,128)S(1)}, s32[]{:T(128)}) %tuple.643), condition=%wide.region_8.9_spmd.clone.clone, body=%wide.region_7.8_spmd.clone.clone.sunk | while | flops 12770 | bytes 53069 | solution.py:69
  329.0 5.6 while.289
  342.5 44.2 %while.298 = (s32[]{:T(128)}, f32[64,32]{0,1:T(8,128)S(1)}, s32[]{:T(128)}) while((s32[]{:T(128)}, f32[64,32]{0,1:T(8,128)S(1)}, s32[]{:T(128)}) %tuple.649), condition=%wide.region_12.13_spmd.clone.clone, body=%wide.region_11.12_spmd.clone.clone.sunk | while | flops 8546 | bytes 36237 | solution.py:69
  386.9 5.6 while.290
  400.1 43.5 %while.299 = (s32[]{:T(128)}, f32[32,32]{0,1:T(8,128)S(1)}, s32[]{:T(128)}) while((s32[]{:T(128)}, f32[32,32]{0,1:T(8,128)S(1)}, s32[]{:T(128)}) %tuple.655), condition=%wide.region_16.17_spmd.clone.clone, body=%wide.region_15.16_spmd.clone.clone.sunk | while | flops 4322 | bytes 19401 | solution.py:69
  446.3 189.2 %while.300 = (s32[]{:T(128)}, f32[128,128]{1,0:T(8,128)S(1)}, f32[128,128]{1,0:T(8,128)S(1)}, f32[128,128]{1,0:T(8,128)S(1)}, s32[]{:T(128)}, /*index=5*/s32[]{:T(128)}, s32[]{:T(128)}, s32[]{:T(128)}) while((s32[]{:T(128)}, f32[128,128]{1,0:T(8,128)S(1)}, f32[128,128]{1,0:T(8,128)S(1)}, f32[128,128]{1,0:T(8,128)S(1)}, ...), condition=%wide.region_19.20_spmd.clone.clone, body=%wide.region_17.19_spmd.clone.clone.sunk | while | flops 197509 | bytes 70303 | solution.py:46
  635.5 26.2 %while.291 = (s32[]{:T(128)}, f32[128,128]{1,0:T(8,128)S(1)}, f32[128,128]{1,0:T(8,128)S(1)}, f32[128,128]{1,0:T(8,128)S(1)}, s32[]{:T(128)}, /*index=5*/s32[]{:T(128)}) while((s32[]{:T(128)}, f32[128,128]{1,0:T(8,128)S(1)}, f32[128,128]{1,0:T(8,128)S(1)}, f32[128,128]{1,0:T(8,128)S(1)}, s32[]{:T(128)}, ...), condition=%wide.region_22.23_spmd.clone, body=%wide.region_21.22_spmd.clone.sunk | while | flops 196994 | bytes 69713 | solution.py:28
  664.8 43.8 %all-reduce.12.cloned.1.call-done = f32[128,256]{1,0:T(8,128)} async-done(((f32[128,256]{1,0:T(8,128)}), f32[128,256]{1,0:T(8,128)}) %all-reduce.12.cloned.1.call-update) | async-done | bytes 131088 | tf_op jit(solution)/shard_map/psum | solution.py:12
  708.6 151.1 %all-reduce.10.cloned.1.call-done = f32[2048,128]{1,0:T(8,128)} async-done(((f32[2048,128]{1,0:T(8,128)}), f32[2048,128]{1,0:T(8,128)}) %all-reduce.10.cloned.1.call-update) | async-done | bytes 1048592 | tf_op jit(solution)/shard_map/psum | solution.py:12
  859.7 3.8 convolution_subtract_fusion.1
  864.2 207.5 %all-reduce.14.cloned.1.call-done = f32[128,128]{1,0:T(8,128)} async-done(((f32[128,128]{1,0:T(8,128)}), f32[128,128]{1,0:T(8,128)}) %all-reduce.14.cloned.1.call-update) | async-done | bytes 65552 | tf_op jit(solution)/shard_map/psum | solution.py:12
  1072.6 47.3 %while.301 = (s32[]{:T(128)}, f32[128,32]{0,1:T(8,128)S(1)}, s32[]{:T(128)}) while((s32[]{:T(128)}, f32[128,32]{0,1:T(8,128)S(1)}, s32[]{:T(128)}) %tuple.664), condition=%wide.region_26.27_spmd.clone.clone, body=%wide.region_25.26_spmd.clone.clone.sunk | while | flops 16994 | bytes 69901 | solution.py:69
  1120.1 5.6 while.292
  1131.6 3.6 scatter.60
  1138.3 47.0 %while.302 = (s32[]{:T(128)}, f32[96,32]{0,1:T(8,128)S(1)}, s32[]{:T(128)}) while((s32[]{:T(128)}, f32[96,32]{0,1:T(8,128)S(1)}, s32[]{:T(128)}) %tuple.670), condition=%wide.region_30.31_spmd.clone.clone, body=%wide.region_29.30_spmd.clone.clone.sunk | while | flops 12770 | bytes 53069 | solution.py:69
  1185.5 5.6 while.293
  1199.0 46.5 %while.303 = (s32[]{:T(128)}, f32[64,32]{0,1:T(8,128)S(1)}, s32[]{:T(128)}) while((s32[]{:T(128)}, f32[64,32]{0,1:T(8,128)S(1)}, s32[]{:T(128)}) %tuple.676), condition=%wide.region_34.35_spmd.clone.clone, body=%wide.region_33.34_spmd.clone.clone.sunk | while | flops 8546 | bytes 36237 | solution.py:69
  1245.7 5.6 while.294
  1259.0 45.8 %while.304 = (s32[]{:T(128)}, f32[32,32]{0,1:T(8,128)S(1)}, s32[]{:T(128)}) while((s32[]{:T(128)}, f32[32,32]{0,1:T(8,128)S(1)}, s32[]{:T(128)}) %tuple.682), condition=%wide.region_38.39_spmd.clone.clone, body=%wide.region_37.38_spmd.clone.clone.sunk | while | flops 4322 | bytes 19401 | solution.py:69
  1307.4 187.1 %while.305 = (s32[]{:T(128)}, f32[128,128]{1,0:T(8,128)S(1)}, f32[128,128]{1,0:T(8,128)S(1)}, f32[128,128]{1,0:T(8,128)S(1)}, s32[]{:T(128)}, /*index=5*/s32[]{:T(128)}, s32[]{:T(128)}, s32[]{:T(128)}) while((s32[]{:T(128)}, f32[128,128]{1,0:T(8,128)S(1)}, f32[128,128]{1,0:T(8,128)S(1)}, f32[128,128]{1,0:T(8,128)S(1)}, ...), condition=%wide.region_41.42_spmd.clone.clone, body=%wide.region_39.41_spmd.clone.clone.sunk | while | flops 197509 | bytes 70303 | solution.py:46
  1494.5 26.2 %while.295 = (s32[]{:T(128)}, f32[128,128]{1,0:T(8,128)S(1)}, f32[128,128]{1,0:T(8,128)S(1)}, f32[128,128]{1,0:T(8,128)S(1)}, s32[]{:T(128)}, /*index=5*/s32[]{:T(128)}) while((s32[]{:T(128)}, f32[128,128]{1,0:T(8,128)S(1)}, f32[128,128]{1,0:T(8,128)S(1)}, f32[128,128]{1,0:T(8,128)S(1)}, s32[]{:T(128)}, ...), condition=%wide.region_44.45_spmd.clone, body=%wide.region_43.44_spmd.clone.sunk | while | flops 196994 | bytes 69713 | solution.py:28
  1524.0 43.7 %all-reduce.18.cloned.1.call-done = f32[128,256]{1,0:T(8,128)} async-done(((f32[128,256]{1,0:T(8,128)}), f32[128,256]{1,0:T(8,128)}) %all-reduce.18.cloned.1.call-update) | async-done | bytes 131088 | tf_op jit(solution)/shard_map/psum | solution.py:12
  1567.7 151.0 %all-reduce.16.cloned.1.call-done = f32[2048,128]{1,0:T(8,128)} async-done(((f32[2048,128]{1,0:T(8,128)}), f32[2048,128]{1,0:T(8,128)}) %all-reduce.16.cloned.1.call-update) | async-done | bytes 1048592 | tf_op jit(solution)/shard_map/psum | solution.py:12
  1718.7 4.4 fusion.172
  1723.0 34.9 %all-reduce.20.cloned.1.call-done = f32[2048,256]{1,0:T(8,128)} async-done(((f32[2048,256]{1,0:T(8,128)}), f32[2048,256]{1,0:T(8,128)}) %all-reduce.20.cloned.1.call-update) | async-done | bytes 2097168 | tf_op jit(solution)/shard_map/psum | solution.py:115
  1758.0 3.0 copy.215
  (3511 shorter events, 869.6 us)
Async XLA Ops:
  6.5 213.3 %all-reduce.8.cloned.1.call-start = ((), (), s32[]{:S(2)}) async-start(), calls=%async_computation | async-start | bytes 131072 | tf_op jit(solution)/shard_map/psum | solution.py:12
  8.5 4.5 copy-start.1
  12.1 650.6 %copy-start = (f32[2048,256]{1,0:T(8,128)}, f32[2048,256]{1,0:T(8,128)S(1)}, u32[]{:S(2)}) copy-start(f32[2048,256]{1,0:T(8,128)S(1)} %fusion.177) | copy-start | bytes 6291460
  12.8 695.8 %all-reduce.12.cloned.1.call-start = ((), (), s32[]{:S(2)}) async-start(), calls=%async_computation.2 | async-start | bytes 262144 | tf_op jit(solution)/shard_map/psum | solution.py:12
  662.6 197.1 %all-reduce.10.cloned.1.call-start = ((), (), s32[]{:S(2)}) async-start(), calls=%async_computation.1 | async-start | bytes 2097152 | tf_op jit(solution)/shard_map/psum | solution.py:12
  664.7 407.0 %all-reduce.14.cloned.1.call-start = ((), (), s32[]{:S(2)}) async-start(), calls=%async_computation.3 | async-start | bytes 131072 | tf_op jit(solution)/shard_map/psum | solution.py:12
  864.2 703.5 %all-reduce.18.cloned.1.call-start = ((), (), s32[]{:S(2)}) async-start(), calls=%async_computation.5 | async-start | bytes 262144 | tf_op jit(solution)/shard_map/psum | solution.py:12
  1521.7 197.0 %all-reduce.16.cloned.1.call-start = ((), (), s32[]{:S(2)}) async-start(), calls=%async_computation.4 | async-start | bytes 2097152 | tf_op jit(solution)/shard_map/psum | solution.py:12
  1523.9 234.1 %all-reduce.20.cloned.1.call-start = ((), (), s32[]{:S(2)}) async-start(), calls=%async_computation.6 | async-start | bytes 4194304 | tf_op jit(solution)/shard_map/psum | solution.py:115
Sparse Core Ops, SparseCore 0:
  13.0 206.8 all-reduce.7
  662.8 45.8 all-reduce.11
  712.1 147.6 all-reduce.9
  865.1 206.6 all-reduce.13
  1521.8 45.8 all-reduce.17
  1571.0 147.6 all-reduce.15
  1723.2 34.7 all-reduce.19
where the time goes:
time: 1780 us; the launch traced here: 1770 us
  waiting for transfers between devices  838 us (47%)
  other arithmetic  353 us (20%)
  matrix products  297 us (17%)
  local copies, waits for them, and re-layouts  244 us (14%)
  loops' own time  21.9 us (1%)
    psum x6, waiting for transfers between devices, spread(): return lax.psum(block, axis)  803 us
    dot_general x256, matrix products, sweep(): jnp.dot(coeffs, result, precision=highest)  202 us
    reduce_sum x256, other arithmetic, sweep(): pivot_value = jnp.sum(jnp.where(places == index, line, 0.0))  160 us
    broadcast_in_dim x256, other arithmetic, sweep(): jnp.where((col_places[None, :] == k) & (row_places[:, None] > k), below_c...  158 us
    dynamic_slice x256, local copies, waits for them, and re-layouts, sweep(): pivot_value = panel[k, k]  152 us
    dot_general x448, matrix products, sweep(): row_new = unit_row - jnp.dot(coeffs, result, precision=highest)  65.4 us
  transfers between devices with their start and end apart: 7, of which 7 were waited for; matrix products, arithmetic and copies ran while one was open for 0% of the time, Pallas kernels for 0%

commit v1 on v0

v1 whole, which is shorter than its diff:
```python
import jax
import jax.numpy as jnp
from jax import lax
from jax.experimental import pallas as pl
from jax.experimental.pallas import tpu as pltpu
from jax.sharding import PartitionSpec as P

B = 128
PIV = 256
ROWS = 2048
COLS = 256
NB = 16
NZ, NY, NX = 8, 4, 4
HALF = ROWS // 2
CHUNKS = 16
CROWS = HALF // CHUNKS
ICHUNKS = 4
IROWS = PIV // 2 // ICHUNKS
LAG = 7
TILE = 256
TILES = ROWS // TILE
MESH = pl.DeviceIdType.MESH


def split(x):
    high = x.astype(jnp.bfloat16)
    low = (x - high.astype(jnp.float32)).astype(jnp.bfloat16)
    return high, low


def dot3(a, b):
    f32 = jnp.float32
    total = jnp.dot(a[1], b[0], preferred_element_type=f32)
    total = total + jnp.dot(a[0], b[1], preferred_element_type=f32)
    return total + jnp.dot(a[0], b[0], preferred_element_type=f32)


def eliminate(rows, first):
    cols = [jnp.broadcast_to(rows[:, first + j : first + j + 1], (NB, B)) for j in range(NB)]
    place = lax.broadcasted_iota(jnp.int32, (NB, B), 0)
    for k in range(NB):
        here = place == k
        column = cols[k]
        recip = 1.0 / jnp.broadcast_to(column[k : k + 1, :], (NB, B))
        for j in range(NB):
            if j != k:
                scaled = jnp.broadcast_to(cols[j][k : k + 1, :], (NB, B)) * recip
                cols[j] = jnp.where(here, scaled, cols[j] - column * scaled)
        cols[k] = jnp.where(here, recip, -column * recip)
    lane = lax.broadcasted_iota(jnp.int32, (NB, PIV), 1)
    row = lax.broadcasted_iota(jnp.int32, (NB, PIV), 0)
    rows = jnp.where((lane >= first) & (lane < first + NB), jnp.where(lane == first + row, 1.0, 0.0), rows)
    total = None
    for j in range(NB):
        term = jnp.concatenate([cols[j]] * (PIV // B), axis=1) * jnp.broadcast_to(rows[j : j + 1, :], (NB, PIV))
        total = term if total is None else total + term
    return total


def invert(block, between):
    lane = lax.broadcasted_iota(jnp.int32, (PIV, PIV), 1)
    for step in range(PIV // NB):
        first = step * NB
        row_part = eliminate(block[first : first + NB, :], first)
        col_part = block[:, first : first + NB]
        rest = jnp.where((lane >= first) & (lane < first + NB), 0.0, block[...])
        block[...] = rest - jnp.dot(
            col_part, row_part, precision=lax.Precision.HIGHEST, preferred_element_type=jnp.float32
        )
        block[first : first + NB, :] = row_part
        between(step)


def kernel(
    front, row_pattern, col_pattern, out,
    panel, mine, above, inverse, peer, total,
    panel_recv, panel_send, inv_recv, inv_send, above_recv, above_send, peer_recv, peer_send,
    out_sem, load_sem,
):
    g = lax.axis_index("grp")
    r = lax.axis_index("row")
    c = lax.axis_index("col")
    z = c // NY
    y = c % NY

    def at(dx=0, dz=0, dy=0):
        zz = lax.rem(z + dz + NZ, NZ)
        yy = lax.rem(y + dy + NY, NY)
        return (g, lax.rem(r + dx + NX, NX), zz * NY + yy)

    other = (1 - g, r, c)
    near = [at(dz=1), at(dz=-1), at(dy=1), at(dy=-1)]
    beside = [at(dx=1), at(dx=2), at(dx=3)]
    targets = near + [at(dx=1), at(dx=-1)]

    barrier = pltpu.get_barrier_semaphore()
    for device in near + beside + [other]:
        pl.semaphore_signal(barrier, inc=1, device_id=device, device_id_type=MESH)

    root = c == 0
    owner = root & (r == 0)
    up = z <= 3
    down = (z == 0) | (z >= 6)
    flags = (
        (
            (y == 0) & up,
            ((y == 0) & down) | ((y != 0) & (z == 1)),
            (z != 0) & (y <= 1),
            (z != 0) & (y == 0),
            root & (r <= 1),
            root & (r == 0),
        ),
        (
            (y != 0) & up,
            (y != 0) & down,
            (z == 0) & (y <= 1),
            root | ((z != 0) & (y == 1)),
            root & (r == 0),
            root & ((r == 0) | (r == 3)),
        ),
    )
    late = (((z == 0) & (y != 0)).astype(jnp.int32), ((y == 0) & (z != 0)).astype(jnp.int32))

    load_mine = pltpu.make_async_copy(front.at[0], mine, load_sem.at[0])
    load_mine.start()
    load_pivot = pltpu.make_async_copy(front.at[0, 0:PIV, :], inverse, load_sem.at[1])
    load_above = pltpu.make_async_copy(front.at[0, 0:PIV, :], above, load_sem.at[2])
    load_panel = pltpu.make_async_copy(front.at[0], panel, load_sem.at[3])

    @pl.when(owner)
    def _():
        load_pivot.start()

    @pl.when(r == 0)
    def _():
        load_above.start()

    @pl.when(root)
    def _():
        load_panel.start()

    pl.semaphore_wait(barrier, len(near) + len(beside) + 1)

    def panel_rows(tree, chunk):
        return pl.ds(tree * HALF + chunk * CROWS, CROWS)

    def send_panel(source, tree, chunk, slot):
        rows = panel_rows(tree, chunk)
        pltpu.make_async_remote_copy(
            source.at[rows, :], panel.at[rows, :], panel_send.at[tree, slot], panel_recv.at[tree, chunk],
            device_id=targets[slot], device_id_type=MESH,
        ).start()

    def root_sends(chunk):
        send_panel(front.at[0], 0, chunk, 0)
        send_panel(front.at[0], 1, chunk, 2)
        send_panel(front.at[0], 0, chunk, 1)
        send_panel(front.at[0], 1, chunk, 3)

    def send_above(slot):
        return pltpu.make_async_remote_copy(
            front.at[0, 0:PIV, :], above, above_send.at[slot], above_recv,
            device_id=beside[slot], device_id_type=MESH,
        )

    @pl.when(r == 0)
    def _():
        for slot in range(3):
            send_above(slot).start()

    def inverse_rows(tree, chunk):
        return pl.ds(tree * (PIV // 2) + chunk * IROWS, IROWS)

    def inverse_copy(tree, chunk, slot):
        rows = inverse_rows(tree, chunk)
        return pltpu.make_async_remote_copy(
            inverse.at[rows, :], inverse.at[rows, :], inv_send.at[tree, slot], inv_recv.at[tree, chunk],
            device_id=targets[slot], device_id_type=MESH,
        )

    @pl.when(owner)
    def _():
        load_pivot.wait()

        def between(step):
            if step < CHUNKS // 2:
                root_sends(2 * step)
                root_sends(2 * step + 1)

        invert(inverse, between)
        for chunk in range(ICHUNKS):
            for slot in (4, 5, 0, 1, 2, 3):
                for tree in range(2):

                    @pl.when(flags[tree][slot])
                    def _(tree=tree, slot=slot, chunk=chunk):
                        inverse_copy(tree, chunk, slot).start()

    @pl.when(root & (r != 0))
    def _():
        def body(chunk, carry):
            root_sends(chunk)
            return carry

        lax.fori_loop(0, CHUNKS, body, 0)

    @pl.when(jnp.logical_not(root))
    def _():
        def body(step, carry):
            for tree in range(2):
                chunk = step - LAG * late[tree]

                @pl.when((chunk >= 0) & (chunk < CHUNKS))
                def _(tree=tree, chunk=chunk):
                    rows = panel_rows(tree, chunk)
                    pltpu.make_async_copy(panel.at[rows, :], panel.at[rows, :], panel_recv.at[tree, chunk]).wait()
                    for slot in range(4):

                        @pl.when(flags[tree][slot])
                        def _(slot=slot):
                            send_panel(panel, tree, chunk, slot)

            return carry

        lax.fori_loop(0, CHUNKS + LAG, body, 0)

    @pl.when(jnp.logical_not(owner))
    def _():
        def body(step, carry):
            for tree in range(2):
                chunk = step - ICHUNKS * late[tree]

                @pl.when((chunk >= 0) & (chunk < ICHUNKS))
                def _(tree=tree, chunk=chunk):
                    rows = inverse_rows(tree, chunk)
                    pltpu.make_async_copy(inverse.at[rows, :], inverse.at[rows, :], inv_recv.at[tree, chunk]).wait()
                    for slot in (4, 5, 0, 1, 2, 3):

                        @pl.when(flags[tree][slot])
                        def _(slot=slot):
                            inverse_copy(tree, chunk, slot).start()

            return carry

        lax.fori_loop(0, 2 * ICHUNKS, body, 0)

    load_mine.wait()

    @pl.when(r == 0)
    def _():
        load_above.wait()

    @pl.when(r != 0)
    def _():
        send_above(0).wait_recv()

    @pl.when(root)
    def _():
        load_panel.wait()

    place = lax.broadcasted_iota(jnp.int32, (PIV, COLS), 0)
    across = lax.broadcasted_iota(jnp.int32, (PIV, COLS), 1)
    keep = jnp.where(
        place < B,
        jnp.where(across < B, col_pattern[0, 2 * c], col_pattern[0, 2 * c + 1]),
        jnp.where(across < B, col_pattern[1, 2 * c], col_pattern[1, 2 * c + 1]),
    )
    right = jnp.where(keep != 0, above[...], 0.0)
    solved = jnp.dot(
        inverse[...], right, precision=lax.Precision.HIGHEST, preferred_element_type=jnp.float32
    )
    solved = split(solved)

    def exchange(tile):
        rows = pl.ds(tile * TILE, TILE)
        return pltpu.make_async_remote_copy(
            mine.at[rows, :], peer.at[rows, :], peer_send, peer_recv.at[tile],
            device_id=other, device_id_type=MESH,
        )

    def store_out(tile):
        rows = pl.ds(tile * TILE, TILE)
        return pltpu.make_async_copy(total.at[rows, :], out.at[rows, :], out_sem)

    for tile in range(TILES + 2):
        if tile < TILES:
            rows = slice(tile * TILE, (tile + 1) * TILE)
            i = r * (ROWS // B) + 2 * tile
            keep = jnp.where(
                place < B,
                jnp.where(across < B, row_pattern[0, i], row_pattern[1, i]),
                jnp.where(across < B, row_pattern[0, i + 1], row_pattern[1, i + 1]),
            )
            left = split(jnp.where(keep != 0, panel[rows, :], 0.0))
            update = mine[rows, :] - dot3(left, solved)
            trailing = jnp.logical_not(root) & (i >= 2)
            mine[rows, :] = jnp.where(trailing, update, 0.0)
            exchange(tile).start()
        if tile >= 2:
            done = tile - 2
            rows = slice(done * TILE, (done + 1) * TILE)
            exchange(done).wait_recv()
            total[rows, :] = mine[rows, :] + peer[rows, :]
            store_out(done).start()

    pltpu.make_async_copy(total, out, out_sem).wait()
    pltpu.make_async_copy(mine, mine, peer_send).wait()

    @pl.when(r == 0)
    def _():
        for slot in range(3):
            send_above(slot).wait_send()

    for tree in range(2):
        half = pl.ds(tree * HALF, HALF)
        part = pl.ds(tree * (PIV // 2), PIV // 2)
        for slot in range(6):

            @pl.when(flags[tree][slot])
            def _(tree=tree, slot=slot, half=half, part=part):
                if slot < 4:
                    pltpu.make_async_copy(panel.at[half, :], panel.at[half, :], panel_send.at[tree, slot]).wait()
                pltpu.make_async_copy(inverse.at[part, :], inverse.at[part, :], inv_send.at[tree, slot]).wait()


def shards(front_matrix, row_pattern, col_pattern):
    f32 = jnp.float32
    dma = pltpu.SemaphoreType.DMA
    return pl.pallas_call(
        kernel,
        out_shape=jax.ShapeDtypeStruct((ROWS, COLS), f32),
        in_specs=[
            pl.BlockSpec(memory_space=pl.ANY),
            pl.BlockSpec(memory_space=pltpu.SMEM),
            pl.BlockSpec(memory_space=pltpu.SMEM),
        ],
        out_specs=pl.BlockSpec(memory_space=pl.ANY),
        scratch_shapes=[
            pltpu.VMEM((ROWS, COLS), f32),
            pltpu.VMEM((ROWS, COLS), f32),
            pltpu.VMEM((PIV, COLS), f32),
            pltpu.VMEM((PIV, PIV), f32),
            pltpu.VMEM((ROWS, COLS), f32),
            pltpu.VMEM((ROWS, COLS), f32),
            dma((2, CHUNKS)),
            dma((2, 4)),
            dma((2, ICHUNKS)),
            dma((2, 6)),
            dma(()),
            dma((3,)),
            dma((TILES,)),
            dma(()),
            dma(()),
            dma((4,)),
        ],
        compiler_params=pltpu.CompilerParams(
            collective_id=0, has_side_effects=True, vmem_limit_bytes=32 * 1024 * 1024
        ),
        cost_estimate=pl.CostEstimate(
            flops=2 * ROWS * COLS * PIV, bytes_accessed=6 * ROWS * COLS * 4, transcendentals=0
        ),
        name="panel_update",
    )(front_matrix, row_pattern, col_pattern)


def solution(mesh):
    in_specs = (P("grp", "row", "col"), P(), P())
    out_specs = P("row", "col")
    return jax.shard_map(shards, mesh=mesh, in_specs=in_specs, out_specs=out_specs, check_vma=False)
```

time: 1780 us -> 63.5 us (0.04)
  the two profiles are of different devices: /device:TPU:37 before, /device:TPU:129 now
where the time goes in v1:
time: 63.5 us; the launch traced here: 63.3 us
  Pallas kernels  59 us (93%)
  local copies, waits for them, and re-layouts  4.27 us (7%)
    pallas_call x1, Pallas kernels, shards(): pl.pallas_call(kernel, out_shape=jax.ShapeDtypeStruct((ROWS, COLS), f32),...  59 us
    unnamed x7, local copies, waits for them, and re-layouts  4.27 us

profile of v1, /device:TPU:129, one launch (start us, length us, event | category | flops | bytes accessed | tf_op | source)
XLA Modules:
  0.0 63.3 jit_solution(12815629074319620484)
XLA Ops:
  0.0 0.0 copy-start
  0.0 1.6 %copy-done = f32[1,2048,256]{2,1,0:T(8,128)S(1)} copy-done((f32[1,2048,256]{2,1,0:T(8,128)S(1)}, f32[1,2048,256]{2,1,0:T(8,128)}, u32[]{:S(2)}) %copy-start) | copy-done | bytes 2097176
  1.6 0.0 copy-start.1
  1.6 0.7 %copy-done.1 = s32[2,64]{1,0:T(2,128)S(1)} copy-done((s32[2,64]{1,0:T(2,128)S(1)}, s32[2,64]{1,0:T(2,128)}, u32[]{:S(2)}) %copy-start.1) | copy-done | bytes 536
  2.3 0.0 copy-start.2
  2.3 0.7 %copy-done.2 = s32[2,64]{1,0:T(2,128)S(1)} copy-done((s32[2,64]{1,0:T(2,128)S(1)}, s32[2,64]{1,0:T(2,128)}, u32[]{:S(2)}) %copy-start.2) | copy-done | bytes 536
  3.0 59.0 %panel_update.1 = f32[2048,256]{1,0:T(8,128)S(1)} custom-call(f32[1,2048,256]{2,1,0:T(8,128)S(1)} %copy-done, s32[2,64]{1,0:T(2,128)S(1)} %copy-done.1, s32[2,64]{1,0:T(2,128)S(1)} %copy-done.2), custom_call_target="tpu_custom_call" | custom-call | flops 268435456 | bytes 12582912 | tf_op jit(solution)/shard_map/panel_update/pallas_call | solution.py:329
  62.0 1.3 %copy.5 = f32[2048,256]{1,0:T(8,128)} copy(f32[2048,256]{1,0:T(8,128)S(1)} %panel_update.1) | data formatting | bytes 4194304
Async XLA Ops:
  0.0 1.6 %copy-start = (f32[1,2048,256]{2,1,0:T(8,128)S(1)}, f32[1,2048,256]{2,1,0:T(8,128)}, u32[]{:S(2)}) copy-start(f32[1,2048,256]{2,1,0:T(8,128)} %front.1) | copy-start | bytes 6291460
  1.6 0.7 %copy-start.1 = (s32[2,64]{1,0:T(2,128)S(1)}, s32[2,64]{1,0:T(2,128)}, u32[]{:S(2)}) copy-start(s32[2,64]{1,0:T(2,128)} %row_pattern.1) | copy-start | bytes 1540
  2.3 0.7 %copy-start.2 = (s32[2,64]{1,0:T(2,128)S(1)}, s32[2,64]{1,0:T(2,128)}, u32[]{:S(2)}) copy-start(s32[2,64]{1,0:T(2,128)} %col_pattern.1) | copy-start | bytes 1540

commit v2 on v1

v2 whole, which is shorter than its diff:
```python
import jax
import jax.numpy as jnp
from jax import lax
from jax.experimental import pallas as pl
from jax.experimental.pallas import tpu as pltpu
from jax.sharding import PartitionSpec as P

B = 128
PIV = 256
ROWS = 2048
COLS = 256
NB = 16
NZ, NY, NX = 8, 4, 4
TREES = 4
QUARTER = ROWS // TREES
CROWS = 16
CHUNKS = QUARTER // CROWS
IQUARTER = PIV // TREES
ICHUNKS = IQUARTER // CROWS
PLACES = CHUNKS + ICHUNKS
SPAN = PLACES * CROWS
AHEAD = CHUNKS * 3 // 4
LEVEL = 80
TILE = 256
TILES = ROWS // TILE
LATER = 3
MESH = pl.DeviceIdType.MESH

STEPS_IN = (
    (0, 1, 2, 3), (1, 0, 2, 3), (1, 0, 2, 3), (1, 0, 2, 3),
    (0, 1, 3, 2), (2, 3, 0, 1), (2, 0, 1, 3), (1, 2, 3, 0),
    (0, 1, 3, 2), (2, 1, 0, 3), (1, 0, 2, 3), (3, 1, 2, 0),
    (0, 1, 3, 2), (2, 1, 0, 3), (3, 1, 2, 0), (3, 1, 2, 0),
    (0, 1, 3, 2), (2, 1, 0, 3), (3, 2, 0, 1), (3, 1, 2, 0),
    (0, 1, 3, 2), (0, 2, 1, 3), (0, 2, 1, 3), (0, 3, 2, 1),
    (0, 1, 3, 2), (0, 2, 1, 3), (1, 0, 2, 3), (0, 3, 2, 1),
    (0, 1, 3, 2), (3, 2, 1, 0), (1, 2, 0, 3), (2, 0, 3, 1),
)


def walk(chip, direction, back=False):
    z, y = divmod(chip, NY)
    move = -1 if back else 1
    dz, dy = ((1, 0), (-1, 0), (0, 1), (0, -1))[direction]
    return (z + move * dz) % NZ * NY + (y + move * dy) % NY


def bits(values):
    word = sum(1 << chip for chip, value in enumerate(values) if value)
    return word - (1 << 32) if word >= 1 << 31 else word


def depth(tree, chip):
    steps = 0
    while chip:
        chip = walk(chip, STEPS_IN[chip][tree], back=True)
        steps += 1
    return steps


PLANE = range(NZ * NY)
DEPTHS = [[depth(tree, chip) for chip in PLANE] for tree in range(TREES)]


def carried(chip, direction):
    child = walk(chip, direction)
    return STEPS_IN[child].index(direction) if child else None


CARRIED = [[carried(n, d) for n in PLANE] for d in range(4)]
OUT = [bits([CARRIED[d][n] is not None for n in PLANE]) for d in range(4)]
TREE_BITS = [[bits([(CARRIED[d][n] or 0) >> b & 1 for n in PLANE]) for b in range(2)] for d in range(4)]
FIRST = [
    bits([CARRIED[d][n] is not None and CARRIED[d][n] not in [CARRIED[e][n] for e in range(d)] for n in PLANE])
    for d in range(4)
]
LEAF = [bits([all(CARRIED[d][n] != t for d in range(4)) for n in PLANE]) for t in range(TREES)]


def behind(chip, direction):
    trees = [CARRIED[d][chip] for d in range(4) if CARRIED[d][chip] is not None]
    mine = CARRIED[direction][chip]
    return 0 if mine is None else DEPTHS[mine][chip] - min(DEPTHS[t][chip] for t in trees)


BEHIND = [[behind(n, d) for n in PLANE] for d in range(4)]
BEHIND_BITS = [[bits([v >> b & 1 for v in BEHIND[d]]) for b in range(3)] for d in range(4)]
LONGEST = max(max(line) for line in BEHIND) * LEVEL // 10
ROOT_WAY = [next(d for d in range(4) if CARRIED[d][0] == t) for t in range(TREES)]


def split(x):
    high = x.astype(jnp.bfloat16)
    low = (x - high.astype(jnp.float32)).astype(jnp.bfloat16)
    return high, low


def stacked_dot(a, b):
    left = jnp.concatenate([a[0], a[0], a[1]], axis=1)
    right = jnp.concatenate([b[0], b[1], b[0]], axis=0)
    return jnp.dot(left, right, preferred_element_type=jnp.float32)


def along(column, width):
    return jnp.concatenate([column] * (width // B), axis=1)


def eliminate(rows, first):
    cols = [jnp.broadcast_to(rows[:, first + j : first + j + 1], (NB, B)) for j in range(NB)]
    place = lax.broadcasted_iota(jnp.int32, (NB, B), 0)
    for k in range(NB):
        here = place == k
        column = cols[k]
        recip = 1.0 / jnp.broadcast_to(column[k : k + 1, :], (NB, B))
        for j in range(NB):
            if j != k:
                scaled = jnp.broadcast_to(cols[j][k : k + 1, :], (NB, B)) * recip
                cols[j] = jnp.where(here, scaled, cols[j] - column * scaled)
        cols[k] = jnp.where(here, recip, -column * recip)
    lane = lax.broadcasted_iota(jnp.int32, (NB, PIV), 1)
    row = lax.broadcasted_iota(jnp.int32, (NB, PIV), 0)
    rows = jnp.where((lane >= first) & (lane < first + NB), jnp.where(lane == first + row, 1.0, 0.0), rows)
    return outer_sum(cols, rows)


def outer_sum(cols, rows):
    total = None
    for j in range(NB):
        term = along(cols[j], PIV) * jnp.broadcast_to(rows[j : j + 1, :], (NB, PIV))
        total = term if total is None else total + term
    return total


def invert(block, between):
    lane = lax.broadcasted_iota(jnp.int32, (PIV, PIV), 1)
    rows = block[0:NB, :]
    for step in range(PIV // NB):
        first = step * NB
        end = first + NB
        row_part = eliminate(rows, first)
        if end < PIV:
            rows = block[end : end + NB, :]
            cols = [jnp.broadcast_to(rows[:, first + j : first + j + 1], (NB, B)) for j in range(NB)]
            rows = jnp.where((lane[:NB] >= first) & (lane[:NB] < end), 0.0, rows) - outer_sum(cols, row_part)
        rest = jnp.where((lane >= first) & (lane < end), 0.0, block[...])
        block[...] = rest - stacked_dot(split(block[:, first:end]), split(row_part))
        block[first:end, :] = row_part
        if end < PIV:
            block[end : end + NB, :] = rows
        between(step)


def kernel(
    front, row_table, col_table, out,
    stream, mine, above, inverse, peer, total, row_pattern, col_pattern,
    recv_sem, send_sem, cross_sem, above_recv, above_send, peer_recv, peer_send, out_sem, load_sem,
):
    g = lax.axis_index("grp")
    r = lax.axis_index("row")
    c = lax.axis_index("col")
    z = c // NY
    y = c % NY

    def at(dx=0, dz=0, dy=0):
        zz = lax.rem(z + dz + NZ, NZ)
        yy = lax.rem(y + dy + NY, NY)
        return (g, lax.rem(r + dx + NX, NX), zz * NY + yy)

    def bit(word):
        return lax.shift_right_logical(jnp.int32(word), c) & 1

    def number(words):
        return sum(bit(word) << place for place, word in enumerate(words))

    other = (1 - g, r, c)
    near = [at(dz=1), at(dz=-1), at(dy=1), at(dy=-1)]
    beside = [at(dx=1), at(dx=2), at(dx=3)]

    barrier = pltpu.get_barrier_semaphore()
    for device in near + beside + [other]:
        pl.semaphore_signal(barrier, inc=1, device_id=device, device_id_type=MESH)

    first_plane = r == 0
    root = c == 0
    owner = root & first_plane
    worker = jnp.logical_not(root)
    out_tree = [number(TREE_BITS[d]) for d in range(4)]
    plus = [root & (first_plane | ((r == 1) if t < 2 else False)) for t in range(TREES)]
    minus = [root & (first_plane | ((r == 3) if t >= 2 else False)) for t in range(TREES)]
    ahead = jnp.where(first_plane, AHEAD, CHUNKS)

    load_pivot = pltpu.make_async_copy(front.at[0, 0:PIV, :], inverse, load_sem.at[1])
    load_mine = pltpu.make_async_copy(front.at[0], mine, load_sem.at[0])
    load_above = pltpu.make_async_copy(front.at[0, 0:PIV, :], above, load_sem.at[2])
    load_rows = pltpu.make_async_copy(row_table, row_pattern, load_sem.at[3])
    load_cols = pltpu.make_async_copy(col_table, col_pattern, load_sem.at[4])

    @pl.when(owner)
    def _():
        load_pivot.start()

    @pl.when(worker)
    def _():
        load_rows.start()
        load_cols.start()
        load_mine.start()

    @pl.when(worker & first_plane)
    def _():
        load_above.start()

    pl.semaphore_wait(barrier, len(near) + len(beside) + 1)

    def places(tree, place):
        return pl.ds(pl.multiple_of(tree * SPAN + place * CROWS, CROWS), CROWS)

    def pass_on(source, tree, place, way):
        pltpu.make_async_remote_copy(
            source, stream.at[places(tree, place), :], send_sem.at[way], recv_sem.at[tree, place],
            device_id=near[way], device_id_type=MESH,
        ).start()

    def take(tree, place):
        rows = places(tree, place)
        pltpu.make_async_copy(stream.at[rows, :], stream.at[rows, :], recv_sem.at[tree, place]).wait()

    def cross(source, tree, chunk, way):
        pltpu.make_async_remote_copy(
            source, stream.at[places(tree, CHUNKS + chunk), :], cross_sem.at[tree, way],
            recv_sem.at[tree, CHUNKS + chunk],
            device_id=(beside[0], beside[2])[way], device_id_type=MESH,
        ).start()

    def root_sends(chunk, place):
        for tree in range(TREES):
            rows = pl.ds(pl.multiple_of(tree * QUARTER + chunk * CROWS, CROWS), CROWS)
            pass_on(front.at[0, rows, :], tree, place, ROOT_WAY[tree])

    def send_above(slot):
        return pltpu.make_async_remote_copy(
            front.at[0, 0:PIV, :], above, above_send.at[slot], above_recv,
            device_id=beside[slot], device_id_type=MESH,
        )

    @pl.when(worker & first_plane)
    def _():
        for slot in range(3):
            send_above(slot).start()

    @pl.when(owner)
    def _():
        load_pivot.wait()
        steps = PIV // NB

        def between(step):
            for chunk in range(step * AHEAD // steps, (step + 1) * AHEAD // steps):
                root_sends(chunk, chunk)

        invert(inverse, between)
        for chunk in range(ICHUNKS):
            for tree in range(TREES):
                source = inverse.at[pl.ds(tree * IQUARTER + chunk * CROWS, CROWS), :]
                cross(source, tree, chunk, 0)
                cross(source, tree, chunk, 1)
                pass_on(source, tree, AHEAD + chunk, ROOT_WAY[tree])
        for chunk in range(AHEAD, CHUNKS):
            root_sends(chunk, chunk + ICHUNKS)

    @pl.when(root & (r != 0))
    def _():
        def body(chunk, carry):
            root_sends(chunk, chunk)
            return carry

        lax.fori_loop(0, CHUNKS, body, 0)
        for chunk in range(ICHUNKS):
            for tree in range(TREES):
                source = stream.at[places(tree, CHUNKS + chunk), :]
                take(tree, CHUNKS + chunk)

                @pl.when(plus[tree])
                def _(source=source, tree=tree, chunk=chunk):
                    cross(source, tree, chunk, 0)

                @pl.when(minus[tree])
                def _(source=source, tree=tree, chunk=chunk):
                    cross(source, tree, chunk, 1)

                pass_on(source, tree, CHUNKS + chunk, ROOT_WAY[tree])

    @pl.when(worker)
    def _():
        leaf = [bit(LEAF[t]) == 1 for t in range(TREES)]
        first = [bit(FIRST[d]) == 1 for d in range(4)]
        starts = [(number(BEHIND_BITS[d]) * LEVEL) // 10 for d in range(4)]
        lengths = [bit(OUT[d]) * PLACES for d in range(4)]

        def body(step, carry):
            for way in range(4):
                place = step - starts[way]

                @pl.when((place >= 0) & (place < lengths[way]))
                def _(way=way, place=place):
                    tree = out_tree[way]

                    @pl.when(first[way])
                    def _():
                        take(tree, place)

                    pass_on(stream.at[places(tree, place), :], tree, place, way)

            return carry

        lax.fori_loop(0, PLACES + LONGEST, body, 0)

        for tree in range(TREES):

            @pl.when(leaf[tree])
            def _(tree=tree):
                def rest(place, carry):
                    take(tree, place)
                    return carry

                lax.fori_loop(0, PLACES, rest, 0)

        load_mine.wait()
        load_rows.wait()
        load_cols.wait()

        @pl.when(first_plane)
        def _():
            load_above.wait()

        @pl.when(r != 0)
        def _():
            send_above(0).wait_recv()

        place = lax.broadcasted_iota(jnp.int32, (PIV, COLS), 0)
        across = lax.broadcasted_iota(jnp.int32, (PIV, COLS), 1)
        keep = jnp.where(
            place < B,
            jnp.where(across < B, col_pattern[0, 2 * c], col_pattern[0, 2 * c + 1]),
            jnp.where(across < B, col_pattern[1, 2 * c], col_pattern[1, 2 * c + 1]),
        )
        right = split(jnp.where(keep != 0, above[...], 0.0))
        solve = jnp.concatenate(
            [
                stream[pl.ds(pl.multiple_of(tree * SPAN + ahead * CROWS, CROWS), IQUARTER), :]
                for tree in range(TREES)
            ],
            axis=0,
        )
        solved = split(stacked_dot(split(solve), right))
        stack = jnp.concatenate([solved[0], solved[1], solved[0]], axis=0)

        def block_row(index):
            chunk = index * B // CROWS % CHUNKS
            start = index * B // QUARTER * SPAN + chunk * CROWS
            if chunk >= AHEAD:
                start = start + jnp.where(first_plane, ICHUNKS * CROWS, 0)
            block = stream[pl.ds(pl.multiple_of(start, CROWS), B), :]
            i = r * (ROWS // B) + index
            keep = jnp.where(across[:B] < B, row_pattern[0, i], row_pattern[1, i])
            return split(jnp.where(keep != 0, block, 0.0))

        def exchange(tile):
            rows = pl.ds(tile * TILE, TILE)
            return pltpu.make_async_remote_copy(
                mine.at[rows, :], peer.at[rows, :], peer_send, peer_recv.at[tile],
                device_id=other, device_id_type=MESH,
            )

        def store_out(tile):
            rows = pl.ds(tile * TILE, TILE)
            return pltpu.make_async_copy(total.at[rows, :], out.at[rows, :], out_sem)

        for tile in range(TILES + LATER):
            if tile < TILES:
                rows = slice(tile * TILE, (tile + 1) * TILE)
                parts = [block_row(tile * (TILE // B) + b) for b in range(TILE // B)]
                high = jnp.concatenate([part[0] for part in parts], axis=0)
                low = jnp.concatenate([part[1] for part in parts], axis=0)
                left = jnp.concatenate([high, high, low], axis=1)
                update = mine[rows, :] - jnp.dot(left, stack, preferred_element_type=jnp.float32)
                if tile == 0:
                    update = jnp.where(r != 0, update, 0.0)
                mine[rows, :] = update
                exchange(tile).start()
            if tile >= LATER:
                done = tile - LATER
                rows = slice(done * TILE, (done + 1) * TILE)
                exchange(done).wait_recv()
                total[rows, :] = mine[rows, :] + peer[rows, :]
                store_out(done).start()

        pltpu.make_async_copy(total, out, out_sem).wait()
        pltpu.make_async_copy(mine, mine, peer_send).wait()

        @pl.when(first_plane)
        def _():
            for slot in range(3):
                send_above(slot).wait_send()

    @pl.when(root)
    def _():
        total[...] = jnp.zeros_like(total)
        clear = pltpu.make_async_copy(total, out, out_sem)
        clear.start()
        clear.wait()

    def sent(rows, semaphore):
        pltpu.make_async_copy(stream.at[0:rows, :], stream.at[0:rows, :], semaphore).wait()

    for way in range(4):

        @pl.when(bit(OUT[way]) == 1)
        def _(way=way):
            sent(SPAN, send_sem.at[way])

    for tree in range(TREES):
        for way, crossed in enumerate((plus[tree], minus[tree])):

            @pl.when(crossed)
            def _(tree=tree, way=way):
                sent(IQUARTER, cross_sem.at[tree, way])


def shards(front_matrix, row_pattern, col_pattern):
    f32, i32 = jnp.float32, jnp.int32
    dma = pltpu.SemaphoreType.DMA
    return pl.pallas_call(
        kernel,
        out_shape=jax.ShapeDtypeStruct((ROWS, COLS), f32),
        in_specs=[pl.BlockSpec(memory_space=pltpu.HBM)] * 3,
        out_specs=pl.BlockSpec(memory_space=pl.ANY),
        scratch_shapes=[
            pltpu.VMEM((TREES * SPAN, COLS), f32),
            pltpu.VMEM((ROWS, COLS), f32),
            pltpu.VMEM((PIV, COLS), f32),
            pltpu.VMEM((PIV, PIV), f32),
            pltpu.VMEM((ROWS, COLS), f32),
            pltpu.VMEM((ROWS, COLS), f32),
            pltpu.SMEM((2, 64), i32),
            pltpu.SMEM((2, 64), i32),
            dma((TREES, PLACES)),
            dma((4,)),
            dma((TREES, 2)),
            dma(()),
            dma((3,)),
            dma((TILES,)),
            dma(()),
            dma(()),
            dma((5,)),
        ],
        compiler_params=pltpu.CompilerParams(
            collective_id=0, has_side_effects=True, vmem_limit_bytes=50 * 1024 * 1024
        ),
        cost_estimate=pl.CostEstimate(
            flops=2 * ROWS * COLS * PIV, bytes_accessed=6 * ROWS * COLS * 4, transcendentals=0
        ),
        name="panel_update",
    )(front_matrix, row_pattern, col_pattern)


def solution(mesh):
    in_specs = (P("grp", "row", "col"), P(), P())
    out_specs = P("row", "col")
    return jax.shard_map(shards, mesh=mesh, in_specs=in_specs, out_specs=out_specs, check_vma=False)
```

time: 63.5 us -> 51.1 us (0.80)
  the two profiles are of different devices: /device:TPU:129 before, /device:TPU:37 now
where the time goes in v2:
time: 51.1 us; the launch traced here: 51 us
  Pallas kernels  48.3 us (95%)
  local copies, waits for them, and re-layouts  2.68 us (5%)
    pallas_call x1, Pallas kernels, shards(): pl.pallas_call(kernel, out_shape=jax.ShapeDtypeStruct((ROWS, COLS), f32),...  48.3 us
    unnamed x5, local copies, waits for them, and re-layouts  2.68 us

profile of v2, /device:TPU:37, one launch (start us, length us, event | category | flops | bytes accessed | tf_op | source)
XLA Modules:
  0.0 51.0 jit_solution(9459241424201232365)
XLA Ops:
  0.0 0.0 copy-start
  0.0 0.7 %copy-done = s32[2,64]{1,0:T(2,128)S(1)} copy-done((s32[2,64]{1,0:T(2,128)S(1)}, s32[2,64]{1,0:T(2,128)}, u32[]{:S(2)}) %copy-start) | copy-done | bytes 536
  0.7 0.0 copy-start.1
  0.7 0.7 %copy-done.1 = s32[2,64]{1,0:T(2,128)S(1)} copy-done((s32[2,64]{1,0:T(2,128)S(1)}, s32[2,64]{1,0:T(2,128)}, u32[]{:S(2)}) %copy-start.1) | copy-done | bytes 536
  1.4 48.3 %panel_update.1 = f32[2048,256]{1,0:T(8,128)S(1)} custom-call(f32[1,2048,256]{2,1,0:T(8,128)} %front.1, s32[2,64]{1,0:T(2,128)S(1)} %copy-done, s32[2,64]{1,0:T(2,128)S(1)} %copy-done.1), custom_call_target="tpu_custom_call" | custom-call | flops 268435456 | bytes 12582912 | tf_op jit(solution)/shard_map/panel_update/pallas_call | solution.py:431
  49.7 1.3 %copy.5 = f32[2048,256]{1,0:T(8,128)} copy(f32[2048,256]{1,0:T(8,128)S(1)} %panel_update.1) | data formatting | bytes 4194304
Async XLA Ops:
  0.0 0.7 %copy-start = (s32[2,64]{1,0:T(2,128)S(1)}, s32[2,64]{1,0:T(2,128)}, u32[]{:S(2)}) copy-start(s32[2,64]{1,0:T(2,128)} %row_table.1) | copy-start | bytes 1540
  0.7 0.7 %copy-start.1 = (s32[2,64]{1,0:T(2,128)S(1)}, s32[2,64]{1,0:T(2,128)}, u32[]{:S(2)}) copy-start(s32[2,64]{1,0:T(2,128)} %col_table.1) | copy-start | bytes 1540

commit v3 on v2

--- a/solution.py
+++ b/solution.py
@@ -20,7 +20,7 @@
 PLACES = CHUNKS + ICHUNKS
 SPAN = PLACES * CROWS
 AHEAD = CHUNKS * 3 // 4
-LEVEL = 80
+LEVEL = 100
 TILE = 256
 TILES = ROWS // TILE
 LATER = 3
@@ -87,6 +87,9 @@
 BEHIND_BITS = [[bits([v >> b & 1 for v in BEHIND[d]]) for b in range(3)] for d in range(4)]
 LONGEST = max(max(line) for line in BEHIND) * LEVEL // 10
 ROOT_WAY = [next(d for d in range(4) if CARRIED[d][0] == t) for t in range(TREES)]
+
+
+INWARD = [(base + step % 2, step // 2) for base in (0, 2) for step in range(2 * ICHUNKS)]
 
 
 def split(x):
@@ -151,8 +154,8 @@
 
 
 def kernel(
-    front, row_table, col_table, out,
-    stream, mine, above, inverse, peer, total, row_pattern, col_pattern,
+    front, table, out,
+    stream, mine, above, inverse, peer, total, patterns,
     recv_sem, send_sem, cross_sem, above_recv, above_send, peer_recv, peer_send, out_sem, load_sem,
 ):
     g = lax.axis_index("grp")
@@ -192,8 +195,7 @@
     load_pivot = pltpu.make_async_copy(front.at[0, 0:PIV, :], inverse, load_sem.at[1])
     load_mine = pltpu.make_async_copy(front.at[0], mine, load_sem.at[0])
     load_above = pltpu.make_async_copy(front.at[0, 0:PIV, :], above, load_sem.at[2])
-    load_rows = pltpu.make_async_copy(row_table, row_pattern, load_sem.at[3])
-    load_cols = pltpu.make_async_copy(col_table, col_pattern, load_sem.at[4])
+    load_table = pltpu.make_async_copy(table, patterns, load_sem.at[3])
 
     @pl.when(owner)
     def _():
@@ -201,8 +203,7 @@
 
     @pl.when(worker)
     def _():
-        load_rows.start()
-        load_cols.start()
+        load_table.start()
         load_mine.start()
 
     @pl.when(worker & first_plane)
@@ -257,12 +258,17 @@
                 root_sends(chunk, chunk)
 
         invert(inverse, between)
-        for chunk in range(ICHUNKS):
-            for tree in range(TREES):
-                source = inverse.at[pl.ds(tree * IQUARTER + chunk * CROWS, CROWS), :]
-                cross(source, tree, chunk, 0)
-                cross(source, tree, chunk, 1)
-                pass_on(source, tree, AHEAD + chunk, ROOT_WAY[tree])
+
+        def quarter(tree, chunk):
+            return inverse.at[pl.ds(tree * IQUARTER + chunk * CROWS, CROWS), :]
+
+        for step in range(TREES * ICHUNKS):
+            tree, chunk = INWARD[step]
+            cross(quarter(tree, chunk), tree, chunk, 0)
+            tree = (tree + 2) % TREES
+            cross(quarter(tree, chunk), tree, chunk, 1)
+            tree, chunk = step % TREES, step // TREES
+            pass_on(quarter(tree, chunk), tree, AHEAD + chunk, ROOT_WAY[tree])
         for chunk in range(AHEAD, CHUNKS):
             root_sends(chunk, chunk + ICHUNKS)
 
@@ -273,20 +279,24 @@
             return carry
 
         lax.fori_loop(0, CHUNKS, body, 0)
-        for chunk in range(ICHUNKS):
-            for tree in range(TREES):
-                source = stream.at[places(tree, CHUNKS + chunk), :]
-                take(tree, CHUNKS + chunk)
-
-                @pl.when(plus[tree])
-                def _(source=source, tree=tree, chunk=chunk):
-                    cross(source, tree, chunk, 0)
-
-                @pl.when(minus[tree])
-                def _(source=source, tree=tree, chunk=chunk):
-                    cross(source, tree, chunk, 1)
-
-                pass_on(source, tree, CHUNKS + chunk, ROOT_WAY[tree])
+
+        for plane in (1, 2, 3):
+
+            @pl.when(r == plane)
+            def _(plane=plane):
+                for step in range(TREES * ICHUNKS):
+                    tree, chunk = INWARD[step]
+                    if plane == 2:
+                        tree, chunk = (0, 2, 1, 3)[step % TREES], step // TREES
+                    if plane == 3:
+                        tree = (tree + 2) % TREES
+                    source = stream.at[places(tree, CHUNKS + chunk), :]
+                    take(tree, CHUNKS + chunk)
+                    if plane == 1 and tree < 2:
+                        cross(source, tree, chunk, 0)
+                    if plane == 3 and tree >= 2:
+                        cross(source, tree, chunk, 1)
+                    pass_on(source, tree, CHUNKS + chunk, ROOT_WAY[tree])
 
     @pl.when(worker)
     def _():
@@ -324,8 +334,7 @@
                 lax.fori_loop(0, PLACES, rest, 0)
 
         load_mine.wait()
-        load_rows.wait()
-        load_cols.wait()
+        load_table.wait()
 
         @pl.when(first_plane)
         def _():
@@ -339,8 +348,8 @@
         across = lax.broadcasted_iota(jnp.int32, (PIV, COLS), 1)
         keep = jnp.where(
             place < B,
-            jnp.where(across < B, col_pattern[0, 2 * c], col_pattern[0, 2 * c + 1]),
-            jnp.where(across < B, col_pattern[1, 2 * c], col_pattern[1, 2 * c + 1]),
+            jnp.where(across < B, patterns[2, 2 * c], patterns[2, 2 * c + 1]),
+            jnp.where(across < B, patterns[3, 2 * c], patterns[3, 2 * c + 1]),
         )
         right = split(jnp.where(keep != 0, above[...], 0.0))
         solve = jnp.concatenate(
@@ -360,7 +369,7 @@
                 start = start + jnp.where(first_plane, ICHUNKS * CROWS, 0)
             block = stream[pl.ds(pl.multiple_of(start, CROWS), B), :]
             i = r * (ROWS // B) + index
-            keep = jnp.where(across[:B] < B, row_pattern[0, i], row_pattern[1, i])
+            keep = jnp.where(across[:B] < B, patterns[0, i], patterns[1, i])
             return split(jnp.where(keep != 0, block, 0.0))
 
         def exchange(tile):
@@ -382,7 +391,7 @@
                 low = jnp.concatenate([part[1] for part in parts], axis=0)
                 left = jnp.concatenate([high, high, low], axis=1)
                 update = mine[rows, :] - jnp.dot(left, stack, preferred_element_type=jnp.float32)
-                if tile == 0:
+                if tile * TILE < PIV:
                     update = jnp.where(r != 0, update, 0.0)
                 mine[rows, :] = update
                 exchange(tile).start()
@@ -431,7 +440,7 @@
     return pl.pallas_call(
         kernel,
         out_shape=jax.ShapeDtypeStruct((ROWS, COLS), f32),
-        in_specs=[pl.BlockSpec(memory_space=pltpu.HBM)] * 3,
+        in_specs=[pl.BlockSpec(memory_space=pltpu.HBM)] * 2,
         out_specs=pl.BlockSpec(memory_space=pl.ANY),
         scratch_shapes=[
             pltpu.VMEM((TREES * SPAN, COLS), f32),
@@ -440,8 +449,7 @@
             pltpu.VMEM((PIV, PIV), f32),
             pltpu.VMEM((ROWS, COLS), f32),
             pltpu.VMEM((ROWS, COLS), f32),
-            pltpu.SMEM((2, 64), i32),
-            pltpu.SMEM((2, 64), i32),
+            pltpu.SMEM((4, 64), i32),
             dma((TREES, PLACES)),
             dma((4,)),
             dma((TREES, 2)),
@@ -450,7 +458,7 @@
             dma((TILES,)),
             dma(()),
             dma(()),
-            dma((5,)),
+            dma((4,)),
         ],
         compiler_params=pltpu.CompilerParams(
             collective_id=0, has_side_effects=True, vmem_limit_bytes=50 * 1024 * 1024
@@ -459,7 +467,7 @@
             flops=2 * ROWS * COLS * PIV, bytes_accessed=6 * ROWS * COLS * 4, transcendentals=0
         ),
         name="panel_update",
-    )(front_matrix, row_pattern, col_pattern)
+    )(front_matrix, jnp.concatenate([row_pattern, col_pattern]))
 
 
 def solution(mesh):

time: 51.1 us -> 49.1 us (0.961)
  local copies, waits for them, and re-layouts: 2.68 us -> 1.32 us
  Pallas kernels: 48.3 us -> 47 us
  other arithmetic: 0 us -> 0.7 us
    unnamed x5 -> x1, local copies, waits for them, and re-layouts: 2.68 us -> 1.32 us
    pallas_call x1, Pallas kernels: 48.3 us -> 47 us  [shards(): pl.pallas_call(kernel, out_shape=jax.ShapeDtypeStruct((ROWS, COLS), f32),...]
    concatenate x0 -> x1, other arithmetic: none -> 0.7 us  [shards(): jnp.concatenate([row_pattern, col_pattern])]
where the time goes in v3:
time: 49.1 us; the launch traced here: 49 us
  Pallas kernels  47 us (96%)
  local copies, waits for them, and re-layouts  1.32 us (3%)
  other arithmetic  0.7 us (1%)
    pallas_call x1, Pallas kernels, shards(): pl.pallas_call(kernel, out_shape=jax.ShapeDtypeStruct((ROWS, COLS), f32),...  47 us
    unnamed x1, local copies, waits for them, and re-layouts  1.32 us

profile of v3, /device:TPU:37, one launch (start us, length us, event | category | flops | bytes accessed | tf_op | source)
XLA Modules:
  0.0 49.0 jit_solution(11282762194725366556)
XLA Ops:
  0.0 0.7 %pad_add_fusion.table = s32[4,64]{1,0:T(4,128)S(1)} fusion(s32[2,64]{1,0:T(2,128)} %param.5, s32[2,64]{1,0:T(2,128)} %param.4), kind=kLoop, calls=%fused_computation | loop fusion | flops 256 | bytes 2048 | tf_op jit(solution)/shard_map/concatenate | solution.py:470
  0.7 47.0 %panel_update.1 = f32[2048,256]{1,0:T(8,128)S(1)} custom-call(f32[1,2048,256]{2,1,0:T(8,128)} %front.1, s32[4,64]{1,0:T(4,128)S(1)} %pad_add_fusion.table), custom_call_target="tpu_custom_call" | custom-call | flops 268435456 | bytes 12582912 | tf_op jit(solution)/shard_map/panel_update/pallas_call | solution.py:440
  47.7 1.3 %copy.5 = f32[2048,256]{1,0:T(8,128)} copy(f32[2048,256]{1,0:T(8,128)S(1)} %panel_update.1) | data formatting | bytes 4194304

commit v4 on v3

--- a/solution.py
+++ b/solution.py
@@ -23,7 +23,7 @@
 LEVEL = 100
 TILE = 256
 TILES = ROWS // TILE
-LATER = 3
+LATER = 5
 MESH = pl.DeviceIdType.MESH
 
 STEPS_IN = (
@@ -114,7 +114,7 @@
     for k in range(NB):
         here = place == k
         column = cols[k]
-        recip = 1.0 / jnp.broadcast_to(column[k : k + 1, :], (NB, B))
+        recip = pl.reciprocal(jnp.broadcast_to(column[k : k + 1, :], (NB, B)))
         for j in range(NB):
             if j != k:
                 scaled = jnp.broadcast_to(cols[j][k : k + 1, :], (NB, B)) * recip

time: 49.1 us -> 49 us (level)
  no operation moved by 1% of the time
where the time goes in v4:
time: 49 us
  Pallas kernels  46.9 us (96%)
  local copies, waits for them, and re-layouts  1.32 us (3%)
  other arithmetic  0.7 us (1%)
    pallas_call x1, Pallas kernels, shards(): pl.pallas_call(kernel, out_shape=jax.ShapeDtypeStruct((ROWS, COLS), f32),...  46.9 us
    unnamed x1, local copies, waits for them, and re-layouts  1.32 us

profile of v4, /device:TPU:37, one launch (start us, length us, event | category | flops | bytes accessed | tf_op | source)
XLA Modules:
  0.0 49.0 jit_solution(2731583484807010092)
XLA Ops:
  0.0 0.7 %pad_add_fusion.table = s32[4,64]{1,0:T(4,128)S(1)} fusion(s32[2,64]{1,0:T(2,128)} %param.5, s32[2,64]{1,0:T(2,128)} %param.4), kind=kLoop, calls=%fused_computation | loop fusion | flops 256 | bytes 2048 | tf_op jit(solution)/shard_map/concatenate | solution.py:470
  0.7 46.9 %panel_update.1 = f32[2048,256]{1,0:T(8,128)S(1)} custom-call(f32[1,2048,256]{2,1,0:T(8,128)} %front.1, s32[4,64]{1,0:T(4,128)S(1)} %pad_add_fusion.table), custom_call_target="tpu_custom_call" | custom-call | flops 268435456 | bytes 12582912 | tf_op jit(solution)/shard_map/panel_update/pallas_call | solution.py:440
  47.6 1.3 %copy.5 = f32[2048,256]{1,0:T(8,128)} copy(f32[2048,256]{1,0:T(8,128)S(1)} %panel_update.1) | data formatting | bytes 4194304
